TPU v7x, 128 devices: a whole 4x4x4 slice. The times are simulated.
128 devices in a mesh: row: 16 (over x, y), col: 8 (over z, core).
Axes of the slice: x: 4, y: 4, z: 4, core: 2. Of those that a mesh axis runs over, the one named last changes fastest.
Arguments:
- tokens: bfloat16 [2048, 4096], P('row', 'col'), may hold values from -6 to 6
- weight_in: bfloat16 [4096, 8192], P('row', 'col'), may hold values from -0.09375 to 0.09375
- weight_out: bfloat16 [8192, 4096], P('row', 'col'), may hold values from -0.0625 to 0.0625
- cotangent: bfloat16 [2048, 4096], P('row', 'col'), may hold values from -3 to 3
Outputs:
- output: bfloat16 [2048, 4096], P('row', 'col')
- grad_tokens: bfloat16 [2048, 4096], P('row', 'col')
- grad_weight_in: bfloat16 [4096, 8192], P('row', 'col')
- grad_weight_out: bfloat16 [8192, 4096], P('row', 'col')
All inputs are finite; a program needn't handle non-finite values.
Results may differ from a plain program's by a relative error of at most 0.005.
Values may be sent and summed in bfloat16 or wider, within the bound.
A program may use at most 128 MiB of HBM per device.

v0:
```python
import math

import jax
import jax.numpy as jnp
from jax import lax
from jax.sharding import PartitionSpec as P

gelu_scale = math.sqrt(2.0 / math.pi)
cubic_term = 0.044715


def activate(preact):
    argument = gelu_scale * (preact + cubic_term * preact * preact * preact)
    return 0.5 * preact * (1.0 + jnp.tanh(argument))


def activate_slope(preact):
    argument = gelu_scale * (preact + cubic_term * preact * preact * preact)
    tanh_value = jnp.tanh(argument)
    return 0.5 * (1.0 + tanh_value) + 0.5 * preact * (
        1.0 - tanh_value * tanh_value
    ) * gelu_scale * (1.0 + 3.0 * cubic_term * preact * preact)


def contract_first(left, right):
    return lax.dot_general(
        left, right, (((0,), (0,)), ((), ())), preferred_element_type=jnp.float32
    )


def contract_last(left, right):
    return lax.dot_general(
        left, right, (((1,), (1,)), ((), ())), preferred_element_type=jnp.float32
    )


def on_device(tokens, weight_in, weight_out, cotangent):
    x_rows = lax.all_gather(tokens, "col", axis=1, tiled=True)
    columns = x_rows
    preact = jnp.dot(
        columns,
        lax.all_gather(weight_in, "row", axis=0, tiled=True),
        preferred_element_type=jnp.float32,
    )
    hidden = activate(preact).astype(jnp.bfloat16)
    hidden_all = lax.all_gather(hidden, "col", axis=1, tiled=True)
    panel = lax.all_gather(weight_out, "row", axis=0, tiled=True)
    columns = hidden_all
    out_sum = jnp.dot(columns, panel, preferred_element_type=jnp.float32)
    block_grad = contract_last(cotangent, panel)
    grad_part = block_grad
    out_sum, grad_part = (out_sum, grad_part)
    output = out_sum.astype(jnp.bfloat16)
    grad_hidden = lax.psum_scatter(grad_part, "col", scatter_dimension=1, tiled=True)
    grad_preact = (grad_hidden * activate_slope(preact)).astype(jnp.bfloat16)
    x_columns = lax.all_to_all(x_rows, "row", split_axis=1, concat_axis=0, tiled=True)
    input_part = contract_last(grad_preact, lax.all_gather(weight_in, "row", axis=0, tiled=True))
    matched = x_columns
    grad_in_sum = contract_first(matched, lax.all_gather(grad_preact, "row", axis=0, tiled=True))
    grad_tokens = lax.psum_scatter(input_part, "col", scatter_dimension=1, tiled=True).astype(
        jnp.bfloat16
    )
    hidden_columns = lax.all_to_all(hidden_all, "row", split_axis=1, concat_axis=0, tiled=True)
    matched = hidden_columns
    grad_out_sum = contract_first(matched, lax.all_gather(cotangent, "row", axis=0, tiled=True))
    return (
        output,
        grad_tokens,
        grad_in_sum.astype(jnp.bfloat16),
        grad_out_sum.astype(jnp.bfloat16),
    )


def solution(mesh):
    placed = (P("row", "col"), P("row", "col"), P("row", "col"), P("row", "col"))
    return jax.shard_map(
        on_device,
        mesh=mesh,
        in_specs=placed,
        out_specs=(P("row", "col"), P("row", "col"), P("row", "col"), P("row", "col")),
        check_vma=False,
    )
```

profile of v0, /device:TPU:1, one launch (start us, length us, event | category | flops | bytes accessed | tf_op | source)
XLA Modules:
  0.0 400.4 jit_solution(11132414045830300287)
XLA Ops:
  7.2 0.7 all-gather.13.cloned.1.call-update
  7.9 0.0 all-gather.7.cloned.1.call-start
  7.9 1.7 copy.11
  9.6 0.0 all-gather.9.cloned.1.call-start
  9.7 0.7 all-gather.9.cloned.1.call-update
  10.4 0.0 reduce-scatter.3.cloned.1.call-start
  10.4 73.6 %all-gather.13.cloned.1.call-done = bf16[8192,512]{1,0:T(8,128)(2,1)} async-done(((bf16[512,512]{1,0:T(8,128)(2,1)}), bf16[8192,512]{1,0:T(8,128)(2,1)}) %all-gather.13.cloned.1.call-update) | async-done | bytes 8388624 | tf_op jit(solution)/shard_map/all_gather | solution.py:47
  84.0 8.2 %fusion.8 = f32[128,8192]{1,0:T(8,128)} fusion(bf16[128,512]{1,0:T(8,128)(2,1)} %param.7, bf16[8192,512]{1,0:T(8,128)(2,1)} %all-gather.13.cloned.1.call-done), kind=kOutput, calls=%fused_computation.15 | convolution fusion | flops 1073741824 | bytes 12713984 | tf_op jit(solution)/shard_map/dot_general | solution.py:32
  92.2 0.0 all-gather.11.cloned.1.call-start
  92.3 17.8 %all-gather.7.cloned.1.call-done = bf16[128,4096]{0,1:T(8,128)(2,1)} async-done(((bf16[128,512]{0,1:T(8,128)(2,1)}), bf16[128,4096]{0,1:T(8,128)(2,1)}) %all-gather.7.cloned.1.call-update) | async-done | bytes 1048592 | tf_op jit(solution)/shard_map/all_gather | solution.py:38
  110.0 72.2 %all-gather.9.cloned.1.call-done = bf16[4096,1024]{1,0:T(8,128)(2,1)} async-done(((bf16[256,1024]{1,0:T(8,128)(2,1)}), bf16[4096,1024]{1,0:T(8,128)(2,1)}) %all-gather.9.cloned.1.call-update) | async-done | bytes 8388624 | tf_op jit(solution)/shard_map/all_gather | solution.py:42
  182.3 37.2 %reduce-scatter.3.cloned.1.call-done = f32[128,1024]{1,0:T(8,128)} async-done(((f32[128,8192]{1,0:T(8,128)}), f32[128,1024]{1,0:T(8,128)}) %reduce-scatter.3.cloned.1.call-update) | async-done | bytes 524304 | tf_op jit(solution)/shard_map/reduce_scatter | solution.py:54
  219.5 6.0 %fusion.7 = (bf16[128,1024]{1,0:T(8,128)(2,1)S(1)}, bf16[128,1024]{1,0:T(8,128)(2,1)}) fusion(f32[128,1024]{1,0:T(8,128)} %reduce-scatter.3.cloned.1.call-done, bf16[128,4096]{0,1:T(8,128)(2,1)} %all-gather.7.cloned.1.call-done, bf16[4096,1024]{1,0:T(8,128)(2,1)} %all-gather.9.cloned.1.call-done), kind=kOutput, calls=%fused_computation.13 | convolution fusion | flops 1076494336 | bytes 10485760 | tf_op jit(solution)/shard_map/dot_general | solution.py:40
  225.6 0.0 reduce-scatter.5.cloned.1.call-start
  225.6 7.6 %fusion.9 = f32[128,4096]{1,0:T(8,128)} fusion(bf16[128,1024]{1,0:T(8,128)(2,1)S(1)} %get-tuple-element.16, bf16[4096,1024]{1,0:T(8,128)(2,1)} %all-gather.9.cloned.1.call-done), kind=kOutput, calls=%fused_computation.16 | convolution fusion | flops 1073741824 | bytes 10747904 | tf_op jit(solution)/shard_map/dot_general | solution.py:32
  233.2 0.0 all-gather.17.cloned.1.call-start
  233.3 0.7 all-gather.17.cloned.1.call-update
  234.0 0.0 all-gather.15.cloned.1.call-start
  234.0 0.7 all-gather.15.cloned.1.call-update
  234.7 6.4 %all-to-all-start = ((bf16[128,16,256]{0,2,1:T(8,128)(2,1)}), bf16[128,16,256]{0,2,1:T(8,128)(2,1)S(1)}, u32[]{:S(2)}, u32[]{:S(2)}) async-start(bf16[128,16,256]{0,2,1:T(8,128)(2,1)} %bitcast), calls=%async_computation.2 | async-start | bytes 2097152 | tf_op jit(solution)/shard_map/all_to_all | solution.py:56
  241.1 12.0 %all-gather.11.cloned.1.call-done = bf16[128,8192]{1,0:T(8,128)(2,1)} async-done(((bf16[128,1024]{1,0:T(8,128)(2,1)}), bf16[128,8192]{1,0:T(8,128)(2,1)}) %all-gather.11.cloned.1.call-update) | async-done | bytes 2097168 | tf_op jit(solution)/shard_map/all_gather | solution.py:46
  253.1 3.2 copy.17
  256.3 6.7 %all-to-all-start.1 = ((bf16[128,16,512]{2,0,1:T(8,128)(2,1)}), bf16[128,16,512]{2,0,1:T(8,128)(2,1)}, u32[]{:S(2)}, u32[]{:S(2)}) async-start(bf16[128,16,512]{2,0,1:T(8,128)(2,1)} %bitcast.25), calls=%async_computation.3 | async-start | bytes 4194304 | tf_op jit(solution)/shard_map/all_to_all | solution.py:63
  263.0 1.3 copy.12
  264.3 5.3 %convolution_convert_fusion.2 = bf16[128,512]{1,0:T(8,128)(2,1)} fusion(bf16[128,8192]{1,0:T(8,128)(2,1)S(1)} %copy-done, bf16[8192,512]{1,0:T(8,128)(2,1)} %all-gather.13.cloned.1.call-done), kind=kOutput, calls=%fused_computation.4 | convolution fusion | flops 1073807360 | bytes 10616832 | tf_op jit(solution)/shard_map/dot_general | solution.py:49
  269.7 17.0 %reduce-scatter.5.cloned.1.call-done = f32[128,512]{1,0:T(8,128)} async-done(((f32[128,4096]{1,0:T(8,128)}), f32[128,512]{1,0:T(8,128)}) %reduce-scatter.5.cloned.1.call-update) | async-done | bytes 262160 | tf_op jit(solution)/shard_map/reduce_scatter | solution.py:60
  286.7 1.6 convert_element_type.24
  288.3 46.4 %all-gather.17.cloned.1.call-done = bf16[2048,512]{1,0:T(8,128)(2,1)} async-done(((bf16[128,512]{1,0:T(8,128)(2,1)}), bf16[2048,512]{1,0:T(8,128)(2,1)}) %all-gather.17.cloned.1.call-update) | async-done | bytes 2097168 | tf_op jit(solution)/shard_map/all_gather | solution.py:65
  334.7 4.3 %convolution_convert_fusion = bf16[512,512]{1,0:T(8,128)(2,1)} fusion(bf16[2048,512]{1,0:T(8,128)(2,1)} %bitcast.5, bf16[2048,512]{1,0:T(8,128)(2,1)} %all-gather.17.cloned.1.call-done), kind=kOutput, calls=%fused_computation.1 | convolution fusion | flops 1074003968 | bytes 4718592 | tf_op jit(solution)/shard_map/dot_general | solution.py:26
  339.0 50.1 %all-gather.15.cloned.1.call-done = bf16[2048,1024]{1,0:T(8,128)(2,1)} async-done(((bf16[128,1024]{1,0:T(8,128)(2,1)}), bf16[2048,1024]{1,0:T(8,128)(2,1)}) %all-gather.15.cloned.1.call-update) | async-done | bytes 4194320 | tf_op jit(solution)/shard_map/all_gather | solution.py:59
  389.1 3.5 fusion
  392.5 1.0 copy.14
  (13 shorter events, 0.1 us)
Async XLA Ops:
  7.2 76.8 %all-gather.13.cloned.1.call-start = ((), (), s32[]{:S(2)}) async-start(), calls=%async_computation.7 | async-start | bytes 8912896 | tf_op jit(solution)/shard_map/all_gather | solution.py:47
  7.9 102.1 %all-gather.7.cloned.1.call-start = ((), (), s32[]{:S(2)}) async-start(), calls=%async_computation.4 | async-start | bytes 1179648 | tf_op jit(solution)/shard_map/all_gather | solution.py:38
  9.6 172.7 %all-gather.9.cloned.1.call-start = ((), (), s32[]{:S(2)}) async-start(), calls=%async_computation.5 | async-start | bytes 8912896 | tf_op jit(solution)/shard_map/all_gather | solution.py:42
  10.4 209.2 %reduce-scatter.3.cloned.1.call-start = ((), (), s32[]{:S(2)}) async-start(), calls=%async_computation.8 | async-start | bytes 4718592 | tf_op jit(solution)/shard_map/reduce_scatter | solution.py:54
  92.2 160.9 %all-gather.11.cloned.1.call-start = ((), (), s32[]{:S(2)}) async-start(), calls=%async_computation.6 | async-start | bytes 2359296 | tf_op jit(solution)/shard_map/all_gather | solution.py:46
  225.5 7.7 %copy-start.1 = (bf16[128,1024]{1,0:T(8,128)(2,1)}, bf16[128,1024]{1,0:T(8,128)(2,1)S(1)}, u32[]{:S(2)}) copy-start(bf16[128,1024]{1,0:T(8,128)(2,1)S(1)} %get-tuple-element.16) | copy-start | bytes 786436
  225.6 61.1 %reduce-scatter.5.cloned.1.call-start = ((), (), s32[]{:S(2)}) async-start(), calls=%async_computation.9 | async-start | bytes 2359296 | tf_op jit(solution)/shard_map/reduce_scatter | solution.py:60
  233.2 101.4 %all-gather.17.cloned.1.call-start = ((), (), s32[]{:S(2)}) async-start(), calls=%async_computation.11 | async-start | bytes 2228224 | tf_op jit(solution)/shard_map/all_gather | solution.py:65
  234.0 155.1 %all-gather.15.cloned.1.call-start = ((), (), s32[]{:S(2)}) async-start(), calls=%async_computation.10 | async-start | bytes 4456448 | tf_op jit(solution)/shard_map/all_gather | solution.py:59
  234.7 21.6 %all-to-all-start = ((bf16[128,16,256]{0,2,1:T(8,128)(2,1)}), bf16[128,16,256]{0,2,1:T(8,128)(2,1)S(1)}, u32[]{:S(2)}, u32[]{:S(2)}) async-start(bf16[128,16,256]{0,2,1:T(8,128)(2,1)} %bitcast), calls=%async_computation.2 | async-start | bytes 2097152 | tf_op jit(solution)/shard_map/all_to_all | solution.py:56
  256.3 8.0 %copy-start = (bf16[128,8192]{1,0:T(8,128)(2,1)S(1)}, bf16[128,8192]{1,0:T(8,128)(2,1)}, u32[]{:S(2)}) copy-start(bf16[128,8192]{1,0:T(8,128)(2,1)} %all-gather.11.cloned.1.call-done) | copy-start | bytes 6291460
  256.3 78.4 %all-to-all-start.1 = ((bf16[128,16,512]{2,0,1:T(8,128)(2,1)}), bf16[128,16,512]{2,0,1:T(8,128)(2,1)}, u32[]{:S(2)}, u32[]{:S(2)}) async-start(bf16[128,16,512]{2,0,1:T(8,128)(2,1)} %bitcast.25), calls=%async_computation.3 | async-start | bytes 4194304 | tf_op jit(solution)/shard_map/all_to_all | solution.py:63
  269.7 119.4 %copy-start.2 = (bf16[16,128,256]{2,1,0:T(8,128)(2,1)S(1)}, bf16[16,128,256]{2,1,0:T(8,128)(2,1)}, u32[]{:S(2)}) copy-start(bf16[16,128,256]{2,1,0:T(8,128)(2,1)} %copy.12) | copy-start | bytes 3145732
Sparse Core Ops, SparseCore 0:
  10.1 73.8 all-gather.12
  86.3 23.7 all-gather.6
  112.2 70.0 all-gather.8
  184.5 34.9 reduce-scatter.2
  225.7 27.3 all-gather.10
  255.4 31.2 reduce-scatter.4
  288.8 45.8 all-gather.16
  337.4 51.6 all-gather.14
where the time goes:
time: 401 us; the launch traced here: 400 us
  waiting for transfers between devices  329 us (82%)
  matrix products  34.9 us (9%)
  between operations  14.2 us (4%)
  starting transfers between devices  13.4 us (3%)
  local copies, waits for them, and re-layouts  7.17 us (2%)
    all_gather x1, waiting for transfers between devices, on_device(): panel = lax.all_gather(weight_out, 'row', axis=0, tiled=True)  73.6 us
    all_gather x1, waiting for transfers between devices, on_device(): lax.all_gather(weight_in, 'row', axis=0, tiled=True)  72.2 us
    all_gather x1, waiting for transfers between devices, on_device(): lax.all_gather(grad_preact, 'row', axis=0, tiled=True)  50.1 us
    all_gather x1, waiting for transfers between devices, on_device(): lax.all_gather(cotangent, 'row', axis=0, tiled=True)  46.4 us
    reduce_scatter x1, waiting for transfers between devices, on_device(): lax.psum_scatter(grad_part, 'col', scatter_dimension=1, tiled=True)  37.2 us
    all_gather x1, waiting for transfers between devices, on_device(): x_rows = lax.all_gather(tokens, 'col', axis=1, tiled=True)  17.8 us
    reduce_scatter x1, waiting for transfers between devices, on_device(): lax.psum_scatter(input_part, 'col', scatter_dimension=1, tiled=True)  17 us
    dot_general x2, matrix products, contract_last(): lax.dot_general(left, right, (((1,), (1,)), ((), ())), preferred_element_...  15.8 us
  transfers between devices with their start and end apart: 10, of which 8 were waited for; matrix products, arithmetic and copies ran while one was open for 8% of the time, Pallas kernels for 0%

commit v1 on v0

v1 whole, which is shorter than its diff:
```python
import functools
import math

import jax
import jax.numpy as jnp
from jax import lax
from jax.experimental import pallas as pl
from jax.experimental.pallas import tpu as pltpu
from jax.sharding import PartitionSpec as P

MESH = pl.DeviceIdType.MESH
BF16 = jnp.bfloat16
F32 = jnp.float32

gelu_scale = math.sqrt(2.0 / math.pi)
cubic_term = 0.044715

chunks = 8
m = 128 // chunks
n = 16 * m
tz = n // 8
W = 512
pieces = 4

relay_gather_1, relay_gather_2 = False, False
relay_sum_z, relay_gather_z = False, False
relay_sum_1, relay_sum_2 = False, False


def activate_both(preact):
    square = preact * preact
    tanh_value = jnp.tanh(gelu_scale * (preact + cubic_term * square * preact))
    half = 0.5 * (1.0 + tanh_value)
    slope = half + 0.5 * preact * (1.0 - tanh_value * tanh_value) * gelu_scale * (
        1.0 + 3.0 * cubic_term * square
    )
    return preact * half, slope


def dot_nn(left, right):
    return jnp.dot(left, right, preferred_element_type=F32)


def dot_nt(left, right):
    return lax.dot_general(
        left, right, (((1,), (1,)), ((), ())), preferred_element_type=F32
    )


def dot_tn(left, right):
    return lax.dot_general(
        left, right, (((0,), (0,)), ((), ())), preferred_element_type=F32
    )


def kernel(
    x_ref, c_ref, win_ref, w2_ref,
    out_ref, gx_ref, gw1_ref, gw2_ref,
    ax, ac, part, ks, kr, zs, zt, zr, hg, os, gs, t1, r1, u, t2, r2, acc,
    w1, gw1, stay, back,
    s_g, r_g, s_k, r_k, s_z, r_z, s_h, r_h, s_p, r_p, s_o, r_o, s_w, r_w,
):
    row, col = lax.axis_index("row"), lax.axis_index("col")
    x, y, z, k = row // 4, lax.rem(row, 4), col // 2, lax.rem(col, 2)
    sign = 1 - 2 * k

    def at(base, step):
        return lax.rem(base + step * sign + 4, 4)

    def on_x(p):
        return (p * 4 + y, col)

    def on_y(p):
        return (x * 4 + p, col)

    def on_z(p):
        return (row, p * 2 + k)

    partner = (row, z * 2 + 1 - k)

    def copy(src, dst, send, recv, device):
        return pltpu.make_async_remote_copy(
            src_ref=src, dst_ref=dst, send_sem=send, recv_sem=recv,
            device_id=device, device_id_type=MESH,
        )

    def shift(b):
        return lax.rem(b + x + y, 4)

    def turn_target(b):
        return (lax.rem(z - shift(b) + 4, 4) * 4 + b, x * 2 + y // 2)

    def turn_source(slot):
        return (z * 4 + 2 * k + slot, lax.rem(x + y + z + 2 * k + slot, 4) * 2 + y // 2)

    home = (x == z) & (lax.rem(x + 2 * y, 4) == 0) & (k == y // 2)

    def is_home(j):
        return home & (lax.rem(y, 2) == j)

    barrier = pltpu.get_barrier_semaphore()

    def greet(device):
        pl.semaphore_signal(barrier, inc=1, device_id=device, device_id_type=MESH)

    for j in (1, 2, 3):
        greet(on_x(lax.rem(x + j, 4)))
        greet(on_y(lax.rem(y + j, 4)))
        greet(on_z(lax.rem(z + j, 4)))
    greet(partner)
    for j in (0, 1):

        @pl.when(jnp.logical_not(is_home(j)))
        def _():
            greet(turn_target(2 * k + j))
            greet(turn_source(j))

    def load(i, _):
        ax[i, x, y] = x_ref[pl.ds(pl.multiple_of(i * m, m), m), :]
        ac[i, x, y] = c_ref[pl.ds(pl.multiple_of(i * m, m), m), :]
        return 0

    lax.fori_loop(0, chunks, load, 0)
    acc[...] = jnp.zeros_like(acc)
    pl.semaphore_wait(barrier, 14 - 2 * home.astype(jnp.int32))

    size = 256 // pieces

    class Turn:
        def __init__(self, way, source, middle, target):
            self.way, self.source, self.middle, self.target = way, source, middle, target

        def move_1(self, j, q):
            where = (self.way, 0, j, q)
            rows = pl.ds(q * size, size)
            return copy(
                self.source(j, rows), self.middle.at[j, rows], s_w.at[where], r_w.at[where],
                on_z(lax.rem(z + shift(2 * k + j), 4)),
            )

        def move_2(self, j, q, slot):
            send, recv = (self.way, 1, j, q), (self.way, 1, slot, q)
            rows = pl.ds(q * size, size)
            return copy(
                self.middle.at[j, rows], self.target(slot, rows),
                s_w.at[send], r_w.at[recv], turn_target(2 * k + j),
            )

        def stay_1(self, j, q):
            rows = pl.ds(q * size, size)
            return pltpu.make_async_copy(
                self.source(j, rows), self.middle.at[j, rows], r_w.at[self.way, 0, j, q]
            )

        def stay_2(self, j, q):
            rows = pl.ds(q * size, size)
            return pltpu.make_async_copy(
                self.middle.at[j, rows], self.target(j, rows), r_w.at[self.way, 1, j, q]
            )

        def either(self, condition, yes, no):
            pl.when(condition)(yes)
            pl.when(jnp.logical_not(condition))(no)

        def start(self):
            for q in range(pieces):
                for j in (0, 1):
                    self.either(
                        shift(2 * k + j) == 0,
                        lambda: self.stay_1(j, q).start(),
                        lambda: self.move_1(j, q).start(),
                    )

        def forward(self):
            slot = lax.rem(y, 2)
            for q in range(pieces):
                for j in (0, 1):
                    self.move_1(j, q).wait_recv()
                    self.either(
                        is_home(j),
                        lambda: self.stay_2(j, q).start(),
                        lambda: self.move_2(j, q, slot).start(),
                    )

        def wait_recv(self):
            for q in range(pieces):
                for slot in (0, 1):
                    self.move_2(0, q, slot).wait_recv()

        def wait_send(self):
            for q in range(pieces):
                for j in (0, 1):
                    pl.when(shift(2 * k + j) != 0)(lambda: self.move_1(j, q).wait_send())
                    pl.when(jnp.logical_not(is_home(j)))(
                        lambda: self.move_2(j, q, 0).wait_send()
                    )

    def half(slot):
        return pl.ds(pl.multiple_of(slot * W, W), W)

    turn_in = Turn(
        0, lambda j, rows: win_ref.at[rows, half(j)], stay, lambda slot, rows: w1.at[slot, rows]
    )
    turn_out = Turn(
        1, lambda j, rows: gw1.at[j, rows], back, lambda slot, rows: gw1_ref.at[rows, half(slot)]
    )

    class Gather:
        def __init__(self, relay, region, place, here, sends, recvs):
            self.relay, self.region, self.place, self.here = relay, region, place, here
            self.sends, self.recvs = sends, recvs

        def move(self, p, step, to):
            j = step % 4
            return copy(
                self.region(p), self.region(p), self.sends.at[j - 1], self.recvs.at[j - 1],
                self.place(at(self.here, to)),
            )

        def start(self):
            if not self.relay:
                self.move(self.here, 2, 2).start()
            self.move(self.here, 1, 1).start()
            self.move(self.here, 3, -1).start()

        def forward(self):
            if self.relay:
                behind = at(self.here, -1)
                self.move(behind, 1, 1).wait_recv()
                self.move(behind, 2, 1).start()

        def wait_recv(self):
            if not self.relay:
                self.move(at(self.here, -1), 1, 1).wait_recv()
            self.move(at(self.here, 1), 3, 1).wait_recv()
            self.move(at(self.here, 2), 2, 1).wait_recv()

        def wait_send(self):
            for j in (1, 2, 3):
                self.move(self.here, j, 1).wait_send()

    class Scatter:
        def __init__(self, relay, source, held, got, place, here, sends, recvs):
            self.relay, self.source, self.held, self.got = relay, source, held, got
            self.place, self.here, self.sends, self.recvs = place, here, sends, recvs

        def move(self, src, step, to):
            j = step % 4
            return copy(
                src, self.got.at[j - 1], self.sends.at[j - 1], self.recvs.at[j - 1],
                self.place(at(self.here, to)),
            )

        def start(self):
            self.move(self.source(at(self.here, 2)), 2, 1 if self.relay else 2).start()
            self.move(self.source(at(self.here, -1)), 3, -1).start()
            if not self.relay:
                self.move(self.source(at(self.here, 1)), 1, 1).start()

        def wait(self, j):
            self.move(self.source(self.here), j, 1).wait_recv()
            return self.got[j - 1].astype(F32)

        def forward(self):
            if self.relay:
                value = self.source(at(self.here, 1))[...].astype(F32) + self.wait(2)
                self.held[...] = value.astype(BF16)
                self.move(self.held, 1, 1).start()

        def total(self, own):
            for j in (3, 1) if self.relay else (1, 3, 2):
                own = own + self.wait(j)
            return own

        def wait_send(self):
            for j in (1, 2, 3):
                self.move(self.source(self.here), j, 1).wait_send()

    def gather_x(i, phase):
        region = (lambda p: ax.at[i, p, y]) if phase == 0 else (lambda p: ax.at[i, :, p])
        place, here = ((on_x, x), (on_y, y))[phase]
        relay = (relay_gather_1, relay_gather_2)[phase]
        return Gather(relay, region, place, here, s_g.at[i, phase, 0], r_g.at[i, phase, 0])

    def gather_c(i, phase):
        region = (lambda p: ac.at[i, x, p]) if phase == 0 else (lambda p: ac.at[i, p])
        place, here = ((on_y, y), (on_x, x))[phase]
        relay = (relay_gather_1, relay_gather_2)[phase]
        return Gather(relay, region, place, here, s_g.at[i, phase, 1], r_g.at[i, phase, 1])

    def gather_h(i):
        return Gather(
            relay_gather_z, lambda p: hg.at[i, :, k, p], on_z, z, s_h.at[i], r_h.at[i]
        )

    def exchange(i, w):
        return copy(ks.at[i, w], kr.at[i, w], s_k.at[i, w], r_k.at[i, w], partner)

    def scatter_z(i, w):
        return Scatter(
            relay_sum_z, lambda p: zs.at[i, w, p], zt.at[i, w], zr.at[i, w], on_z, z,
            s_z.at[i, w], r_z.at[i, w],
        )

    def pair(i, j, p, core):
        return copy(
            hg.at[i, :, core, p], hg.at[i, :, core, p], s_p.at[i, j], r_p.at[i, j], partner
        )

    def scatter_1(i, a):
        source = (lambda p: os.at[i, :, p]) if a == 0 else (lambda p: gs.at[i, p])
        place, here = ((on_y, y), (on_x, x))[a]
        return Scatter(
            relay_sum_1, source, t1.at[i, a], r1.at[i, a], place, here,
            s_o.at[i, 0, a], r_o.at[i, 0, a],
        )

    def scatter_2(i, a):
        place, here = ((on_x, x), (on_y, y))[a]
        return Scatter(
            relay_sum_2, lambda p: u.at[i, a, p], t2.at[i, a], r2.at[i, a], place, here,
            s_o.at[i, 1, a], r_o.at[i, 1, a],
        )

    def gather_1(i):
        gather_x(i, 0).start()
        gather_c(i, 0).start()

    def gather_1_relay(i):
        gather_x(i, 0).forward()
        gather_c(i, 0).forward()

    def gather_2(i):
        gather_x(i, 0).wait_recv()
        gather_x(i, 1).start()
        gather_c(i, 0).wait_recv()
        gather_c(i, 1).start()

    def gather_2_relay(i):
        gather_x(i, 1).forward()
        gather_c(i, 1).forward()

    def give(i, w, product):
        part[i, w] = product.reshape(2, 4, tz, W)
        ks[i, w] = part[i, w, 1 - k]
        exchange(i, w).start()

    def multiply_g(i):
        gather_c(i, 1).wait_recv()
        give(i, 1, dot_nt(ac[i].reshape(n, W), w2_ref[...]))

    def multiply_p(i):
        @pl.when(i == 0)
        def _():
            turn_in.wait_recv()

        gather_x(i, 1).wait_recv()
        give(i, 0, dot_nn(ax[i].reshape(n, W), w1[...].reshape(W, W)))

    def sum_z(i, w):
        exchange(i, w).wait_recv()
        part[i, w, k] += kr[i, w]
        for p in range(4):
            zs[i, w, p] = part[i, w, k, p].astype(BF16)
        scatter_z(i, w).start()

    def sum_z_p(i):
        sum_z(i, 0)

    def sum_z_g(i):
        sum_z(i, 1)

    def sum_z_p_relay(i):
        scatter_z(i, 0).forward()

    def sum_z_g_relay(i):
        scatter_z(i, 1).forward()

    def activate(i):
        grad = scatter_z(i, 1).total(part[i, 1, k, z])
        hidden, slope = activate_both(scatter_z(i, 0).total(part[i, 0, k, z]))
        hg[i, 0, k, z] = hidden.astype(BF16)
        hg[i, 1, k, z] = (grad * slope).astype(BF16)
        gather_h(i).start()
        pair(i, 0, z, k).start()

    def gather_z_relay(i):
        gather_h(i).forward()
        if relay_gather_z:
            pair(i, 1, at(z, -1), k).start()

    def gather_z(i):
        gather_h(i).wait_recv()
        if not relay_gather_z:
            pair(i, 1, at(z, -1), k).start()
        pair(i, 2, at(z, 1), k).start()
        pair(i, 3, at(z, 2), k).start()

    def multiply_2(i):
        pair(i, 0, z, 1 - k).wait_recv()
        pair(i, 1, at(z, 1), 1 - k).wait_recv()
        pair(i, 2, at(z, -1), 1 - k).wait_recv()
        pair(i, 3, at(z, 2), 1 - k).wait_recv()
        product = dot_nn(hg[i, 0].reshape(n, W), w2_ref[...])
        os[i] = product.astype(BF16).reshape(4, 4, m, W)
        scatter_1(i, 0).start()
        product = dot_nt(hg[i, 1].reshape(n, W), w1[...].reshape(W, W))
        gs[i] = product.astype(BF16).reshape(4, 4, m, W)
        scatter_1(i, 1).start()

    def multiply_3(i):
        acc[0] += dot_tn(ax[i].reshape(n, W), hg[i, 1].reshape(n, W))

        @pl.when(i == chunks - 1)
        def _():
            gw1[...] = acc[0].astype(BF16).reshape(2, 256, W)
            turn_out.start()

        acc[1] += dot_tn(hg[i, 0].reshape(n, W), ac[i].reshape(n, W))

    def sum_1_relay(i):
        scatter_1(i, 0).forward()
        scatter_1(i, 1).forward()

    def sum_2(i):
        u[i, 0] = scatter_1(i, 0).total(os[i, :, y].astype(F32)).astype(BF16)
        scatter_2(i, 0).start()
        u[i, 1] = scatter_1(i, 1).total(gs[i, x].astype(F32)).astype(BF16)
        scatter_2(i, 1).start()

    def sum_2_relay(i):
        scatter_2(i, 0).forward()
        scatter_2(i, 1).forward()

    def store(i):
        rows = pl.ds(pl.multiple_of(i * m, m), m)
        out_ref[rows, :] = scatter_2(i, 0).total(u[i, 0, x].astype(F32)).astype(BF16)
        gx_ref[rows, :] = scatter_2(i, 1).total(u[i, 1, y].astype(F32)).astype(BF16)

    def turn_in_relay(i):
        @pl.when(i == 0)
        def _():
            turn_in.forward()

    def turn_out_relay(i):
        @pl.when(i == chunks - 1)
        def _():
            turn_out.forward()

    plan = [
        (14, store),
        (12, sum_2),
        (12, turn_out_relay),
        (10, multiply_2),
        (10, multiply_3),
        (9, gather_z),
        (7, activate),
        (5, sum_z_p),
        (5, sum_z_g),
        (4, multiply_p),
        (4, multiply_g),
        (2, turn_in_relay),
        (2, gather_2),
        (0, gather_1),
    ]

    turn_in.start()

    def tick(now, _):
        for offset, stage in plan:
            i = now - offset

            @pl.when((i >= 0) & (i < chunks))
            def _():
                stage(i)

        return 0

    lax.fori_loop(0, chunks + max(offset for offset, _ in plan), tick, 0)

    gw2_ref[...] = acc[1].astype(BF16)

    def drain(i, _):
        for phase in (0, 1):
            gather_x(i, phase).wait_send()
            gather_c(i, phase).wait_send()
        gather_h(i).wait_send()
        for a in (0, 1):
            exchange(i, a).wait_send()
            scatter_z(i, a).wait_send()
            scatter_1(i, a).wait_send()
            scatter_2(i, a).wait_send()
        for j in range(4):
            pair(i, j, z, k).wait_send()
        return 0

    lax.fori_loop(0, chunks, drain, 0)
    turn_in.wait_send()
    turn_out.wait_recv()
    turn_out.wait_send()


def fused(tokens, cotangent, weight_in, weight_out):
    dma = pltpu.SemaphoreType.DMA
    vmem = pl.BlockSpec(memory_space=pltpu.VMEM)
    anywhere = pl.BlockSpec(memory_space=pl.ANY)
    return pl.pallas_call(
        kernel,
        out_shape=(
            jax.ShapeDtypeStruct((128, W), BF16),
            jax.ShapeDtypeStruct((128, W), BF16),
            jax.ShapeDtypeStruct((256, 2 * W), BF16),
            jax.ShapeDtypeStruct((W, W), BF16),
        ),
        in_specs=[vmem, vmem, anywhere, vmem],
        out_specs=(vmem,) * 4,
        scratch_shapes=[
            pltpu.VMEM((chunks, 4, 4, m, W), BF16),
            pltpu.VMEM((chunks, 4, 4, m, W), BF16),
            pltpu.VMEM((chunks, 2, 2, 4, tz, W), F32),
            pltpu.VMEM((chunks, 2, 4, tz, W), F32),
            pltpu.VMEM((chunks, 2, 4, tz, W), F32),
            pltpu.VMEM((chunks, 2, 4, tz, W), BF16),
            pltpu.VMEM((chunks, 2, tz, W), BF16),
            pltpu.VMEM((chunks, 2, 3, tz, W), BF16),
            pltpu.VMEM((chunks, 2, 2, 4, tz, W), BF16),
            pltpu.VMEM((chunks, 4, 4, m, W), BF16),
            pltpu.VMEM((chunks, 4, 4, m, W), BF16),
            pltpu.VMEM((chunks, 2, 4, m, W), BF16),
            pltpu.VMEM((chunks, 2, 3, 4, m, W), BF16),
            pltpu.VMEM((chunks, 2, 4, m, W), BF16),
            pltpu.VMEM((chunks, 2, m, W), BF16),
            pltpu.VMEM((chunks, 2, 3, m, W), BF16),
            pltpu.VMEM((2, W, W), F32),
            pltpu.VMEM((2, 256, W), BF16),
            pltpu.VMEM((2, 256, W), BF16),
            pltpu.VMEM((2, 256, W), BF16),
            pltpu.VMEM((2, 256, W), BF16),
            dma((chunks, 2, 2, 3)), dma((chunks, 2, 2, 3)),
            dma((chunks, 2)), dma((chunks, 2)),
            dma((chunks, 2, 3)), dma((chunks, 2, 3)),
            dma((chunks, 3)), dma((chunks, 3)),
            dma((chunks, 4)), dma((chunks, 4)),
            dma((chunks, 2, 2, 3)), dma((chunks, 2, 2, 3)),
            dma((2, 2, 2, pieces)), dma((2, 2, 2, pieces)),
        ],
        compiler_params=pltpu.CompilerParams(
            collective_id=0, has_side_effects=True, vmem_limit_bytes=56 << 20
        ),
        cost_estimate=pl.CostEstimate(
            flops=6 * 2 * 2048 * W * W, bytes_accessed=3 << 20, transcendentals=2048 * W
        ),
    )(tokens, cotangent, weight_in, weight_out)


def on_device(tokens, weight_in, weight_out, cotangent):
    return fused(tokens, cotangent, weight_in, weight_out)


def solution(mesh):
    placed = (P("row", "col"),) * 4
    return jax.shard_map(
        on_device, mesh=mesh, in_specs=placed, out_specs=placed, check_vma=False
    )
```

time: 401 us -> 111 us (0.28)
  waiting for transfers between devices: 329 us -> 0 us
  Pallas kernels: 0 us -> 105 us
  matrix products: 34.9 us -> 0 us
  between operations: 14.2 us -> 0.65 us
  starting transfers between devices: 13.4 us -> 0 us
    all_gather x6 -> x0, waiting for transfers between devices: 272 us -> none  [the longest x1 73.6 us: on_device(): panel = lax.all_gather(weight_out, 'row', axis=0, tiled=True)]
    pallas_call x0 -> x1, Pallas kernels: none -> 105 us  [fused(): pl.pallas_call(kernel, out_shape=(jax.ShapeDtypeStruct((128, W), BF16), j...]
    reduce_scatter x2 -> x0, waiting for transfers between devices: 54.3 us -> none  [the longest x1 37.2 us: on_device(): lax.psum_scatter(grad_part, 'col', scatter_dimension=1, tiled=True)]
    dot_general x6 -> x0, matrix products: 34.9 us -> none  [the longest x2 15.8 us: contract_last(): lax.dot_general(left, right, (((1,), (1,)), ((), ())), preferred_element_...]
    all_to_all x2 -> x0, starting transfers between devices: 13.1 us -> none  [the longest x1 6.71 us: on_device(): lax.all_to_all(hidden_all, 'row', split_axis=1, concat_axis=0, tiled=True)]
    all_to_all x2 -> x0, local copies, waits for them, and re-layouts: 4.49 us -> none  [the longest x1 3.18 us: on_device(): lax.all_to_all(hidden_all, 'row', split_axis=1, concat_axis=0, tiled=True)]
  transfers between devices with their start and end apart: 10 -> 0, of which waited for: 8 -> 0; matrix products, arithmetic and copies ran while one was open for 8% -> 0% of each run, Pallas kernels for 0% -> 0%
where the time goes in v1:
time: 111 us
  Pallas kernels  105 us (95%)
  local copies, waits for them, and re-layouts  5.22 us (5%)
    pallas_call x1, Pallas kernels, fused(): pl.pallas_call(kernel, out_shape=(jax.ShapeDtypeStruct((128, W), BF16), j...  105 us
    unnamed x8, local copies, waits for them, and re-layouts  5.22 us

profile of v1, /device:TPU:1, one launch (start us, length us, event | category | flops | bytes accessed | tf_op | source)
XLA Modules:
  0.0 111.1 jit_solution(11693241175350316349)
XLA Ops:
  0.6 105.3 %shard_map.75 = (bf16[128,512]{1,0:T(8,128)(2,1)}, bf16[128,512]{1,0:T(8,128)(2,1)}, bf16[256,1024]{1,0:T(8,128)(2,1)}, bf16[512,512]{1,0:T(8,128)(2,1)}) custom-call(bf16[128,512]{1,0:T(8,128)(2,1)} %x_ref.1, bf16[128,512]{1,0:T(8,128)(2,1)} %c_ref.1, bf16[256,1024]{1,0:T(8,128)(2,1)} %win_ref.1, bf16[512,512]{1,0:T(8,128)(2,1)} %w2_ref.1), custom_call_target="tpu_custom_call" | custom-call | flops 6442450944 | bytes 3145728 | tf_op jit(solution)/shard_map/pallas_call | solution.py:507
  105.9 0.0 copy-start.1
  105.9 1.6 %copy.12 = bf16[128,512]{1,0:T(8,128)(2,1)} copy(bf16[128,512]{1,0:T(8,128)(2,1)} %get-tuple-element.8) | data formatting | bytes 262144
  107.5 1.6 %copy.13 = bf16[128,512]{1,0:T(8,128)(2,1)} copy(bf16[128,512]{1,0:T(8,128)(2,1)} %get-tuple-element.9) | data formatting | bytes 262144
  109.1 0.0 copy-done.1
  109.1 0.0 copy-start
  109.1 0.8 copy.14
  109.9 0.4 copy-done
  110.3 0.8 copy.15
Async XLA Ops:
  105.9 3.2 %copy-start.1 = (bf16[256,1024]{1,0:T(8,128)(2,1)S(1)}, bf16[256,1024]{1,0:T(8,128)(2,1)}, u32[]{:S(2)}) copy-start(bf16[256,1024]{1,0:T(8,128)(2,1)} %get-tuple-element.10) | copy-start | bytes 1572868
  109.1 1.2 %copy-start = (bf16[512,512]{1,0:T(8,128)(2,1)S(1)}, bf16[512,512]{1,0:T(8,128)(2,1)}, u32[]{:S(2)}) copy-start(bf16[512,512]{1,0:T(8,128)(2,1)} %get-tuple-element.11) | copy-start | bytes 1572868

commit v2 on v1

--- a/solution.py
+++ b/solution.py
@@ -20,11 +20,12 @@
 n = 16 * m
 tz = n // 8
 W = 512
+parts_of_result = 2
 pieces = 4
 
 relay_gather_1, relay_gather_2 = False, False
-relay_sum_z, relay_gather_z = False, False
-relay_sum_1, relay_sum_2 = False, False
+relay_sum_z, relay_gather_z = True, True
+relay_sum_1, relay_sum_2 = True, False
 
 
 def activate_both(preact):
@@ -54,11 +55,11 @@
 
 
 def kernel(
-    x_ref, c_ref, win_ref, w2_ref,
+    x_ref, c_ref, win_ref, wout_ref,
     out_ref, gx_ref, gw1_ref, gw2_ref,
     ax, ac, part, ks, kr, zs, zt, zr, hg, os, gs, t1, r1, u, t2, r2, acc,
-    w1, gw1, stay, back,
-    s_g, r_g, s_k, r_k, s_z, r_z, s_h, r_h, s_p, r_p, s_o, r_o, s_w, r_w,
+    w1, w2, gw1, gw2, stay, back, ready,
+    s_g, r_g, s_k, r_k, s_z, r_z, s_h, r_h, s_p, r_p, s_o, r_o, s_w, r_w, s_l, r_l,
 ):
     row, col = lax.axis_index("row"), lax.axis_index("col")
     x, y, z, k = row // 4, lax.rem(row, 4), col // 2, lax.rem(col, 2)
@@ -115,13 +116,16 @@
             greet(turn_target(2 * k + j))
             greet(turn_source(j))
 
-    def load(i, _):
-        ax[i, x, y] = x_ref[pl.ds(pl.multiple_of(i * m, m), m), :]
-        ac[i, x, y] = c_ref[pl.ds(pl.multiple_of(i * m, m), m), :]
-        return 0
-
-    lax.fori_loop(0, chunks, load, 0)
+    loads = [
+        pltpu.make_async_copy(x_ref, ax.at[:, x, y], s_l.at[0]),
+        pltpu.make_async_copy(c_ref, ac.at[:, x, y], s_l.at[1]),
+        pltpu.make_async_copy(wout_ref, w2, s_l.at[2]),
+    ]
+    for one in loads:
+        one.start()
     acc[...] = jnp.zeros_like(acc)
+    loads[0].wait()
+    loads[1].wait()
     pl.semaphore_wait(barrier, 14 - 2 * home.astype(jnp.int32))
 
     size = 256 // pieces
@@ -322,22 +326,24 @@
             s_o.at[i, 1, a], r_o.at[i, 1, a],
         )
 
-    def gather_1(i):
+    def gather_1x(i):
         gather_x(i, 0).start()
+
+    def gather_1c(i):
         gather_c(i, 0).start()
 
-    def gather_1_relay(i):
-        gather_x(i, 0).forward()
-        gather_c(i, 0).forward()
-
-    def gather_2(i):
+    def gather_2x(i):
         gather_x(i, 0).wait_recv()
         gather_x(i, 1).start()
+
+    def gather_2c(i):
         gather_c(i, 0).wait_recv()
         gather_c(i, 1).start()
 
-    def gather_2_relay(i):
+    def gather_2x_relay(i):
         gather_x(i, 1).forward()
+
+    def gather_2c_relay(i):
         gather_c(i, 1).forward()
 
     def give(i, w, product):
@@ -346,8 +352,12 @@
         exchange(i, w).start()
 
     def multiply_g(i):
+        @pl.when(i == 0)
+        def _():
+            loads[2].wait()
+
         gather_c(i, 1).wait_recv()
-        give(i, 1, dot_nt(ac[i].reshape(n, W), w2_ref[...]))
+        give(i, 1, dot_nt(ac[i].reshape(n, W), w2[...]))
 
     def multiply_p(i):
         @pl.when(i == 0)
@@ -396,19 +406,11 @@
         pair(i, 2, at(z, 1), k).start()
         pair(i, 3, at(z, 2), k).start()
 
-    def multiply_2(i):
+    def multiply_w(i):
         pair(i, 0, z, 1 - k).wait_recv()
         pair(i, 1, at(z, 1), 1 - k).wait_recv()
         pair(i, 2, at(z, -1), 1 - k).wait_recv()
         pair(i, 3, at(z, 2), 1 - k).wait_recv()
-        product = dot_nn(hg[i, 0].reshape(n, W), w2_ref[...])
-        os[i] = product.astype(BF16).reshape(4, 4, m, W)
-        scatter_1(i, 0).start()
-        product = dot_nt(hg[i, 1].reshape(n, W), w1[...].reshape(W, W))
-        gs[i] = product.astype(BF16).reshape(4, 4, m, W)
-        scatter_1(i, 1).start()
-
-    def multiply_3(i):
         acc[0] += dot_tn(ax[i].reshape(n, W), hg[i, 1].reshape(n, W))
 
         @pl.when(i == chunks - 1)
@@ -416,26 +418,43 @@
             gw1[...] = acc[0].astype(BF16).reshape(2, 256, W)
             turn_out.start()
 
+    def multiply_o(i):
+        product = dot_nn(hg[i, 0].reshape(n, W), w2[...])
+        os[i] = product.astype(BF16).reshape(4, 4, m, W)
+        scatter_1(i, 0).start()
+
+    def multiply_x(i):
+        product = dot_nt(hg[i, 1].reshape(n, W), w1[...].reshape(W, W))
+        gs[i] = product.astype(BF16).reshape(4, 4, m, W)
+        scatter_1(i, 1).start()
+
+    def multiply_v(i):
         acc[1] += dot_tn(hg[i, 0].reshape(n, W), ac[i].reshape(n, W))
 
-    def sum_1_relay(i):
+    def sum_1o_relay(i):
         scatter_1(i, 0).forward()
+
+    def sum_1x_relay(i):
         scatter_1(i, 1).forward()
 
-    def sum_2(i):
+    def sum_2o(i):
         u[i, 0] = scatter_1(i, 0).total(os[i, :, y].astype(F32)).astype(BF16)
         scatter_2(i, 0).start()
+
+    def sum_2x(i):
         u[i, 1] = scatter_1(i, 1).total(gs[i, x].astype(F32)).astype(BF16)
         scatter_2(i, 1).start()
 
-    def sum_2_relay(i):
-        scatter_2(i, 0).forward()
-        scatter_2(i, 1).forward()
-
-    def store(i):
-        rows = pl.ds(pl.multiple_of(i * m, m), m)
-        out_ref[rows, :] = scatter_2(i, 0).total(u[i, 0, x].astype(F32)).astype(BF16)
-        gx_ref[rows, :] = scatter_2(i, 1).total(u[i, 1, y].astype(F32)).astype(BF16)
+    def keep(i, a):
+        return pltpu.make_async_copy(ready.at[a, i], (out_ref, gx_ref)[a].at[i], r_l.at[a, i])
+
+    def store_o(i):
+        ready[0, i] = scatter_2(i, 0).total(u[i, 0, x].astype(F32)).astype(BF16)
+        keep(i, 0).start()
+
+    def store_x(i):
+        ready[1, i] = scatter_2(i, 1).total(u[i, 1, y].astype(F32)).astype(BF16)
+        keep(i, 1).start()
 
     def turn_in_relay(i):
         @pl.when(i == 0)
@@ -448,20 +467,31 @@
             turn_out.forward()
 
     plan = [
-        (14, store),
-        (12, sum_2),
-        (12, turn_out_relay),
-        (10, multiply_2),
-        (10, multiply_3),
-        (9, gather_z),
-        (7, activate),
-        (5, sum_z_p),
-        (5, sum_z_g),
-        (4, multiply_p),
-        (4, multiply_g),
-        (2, turn_in_relay),
-        (2, gather_2),
-        (0, gather_1),
+        (17, multiply_o),
+        (17, multiply_x),
+        (11, sum_z_g_relay),
+        (14, gather_z_relay),
+        (24, multiply_v),
+        (1, gather_1x),
+        (25, sum_2o),
+        (16, multiply_w),
+        (19, sum_1o_relay),
+        (12, activate),
+        (9, multiply_p),
+        (24, sum_2x),
+        (9, multiply_g),
+        (41, store_o),
+        (19, sum_1x_relay),
+        (20, turn_out_relay),
+        (6, gather_2x),
+        (9, sum_z_p),
+        (9, sum_z_g),
+        (37, store_x),
+        (15, gather_z),
+        (1, gather_1c),
+        (10, sum_z_p_relay),
+        (6, gather_2c),
+        (6, turn_in_relay),
     ]
 
     turn_in.start()
@@ -478,7 +508,9 @@
 
     lax.fori_loop(0, chunks + max(offset for offset, _ in plan), tick, 0)
 
-    gw2_ref[...] = acc[1].astype(BF16)
+    keep_w = pltpu.make_async_copy(gw2, gw2_ref, s_l.at[3])
+    gw2[...] = acc[1].astype(BF16)
+    keep_w.start()
 
     def drain(i, _):
         for phase in (0, 1):
@@ -486,6 +518,7 @@
             gather_c(i, phase).wait_send()
         gather_h(i).wait_send()
         for a in (0, 1):
+            keep(i, a).wait()
             exchange(i, a).wait_send()
             scatter_z(i, a).wait_send()
             scatter_1(i, a).wait_send()
@@ -498,22 +531,22 @@
     turn_in.wait_send()
     turn_out.wait_recv()
     turn_out.wait_send()
+    keep_w.wait()
 
 
 def fused(tokens, cotangent, weight_in, weight_out):
     dma = pltpu.SemaphoreType.DMA
-    vmem = pl.BlockSpec(memory_space=pltpu.VMEM)
     anywhere = pl.BlockSpec(memory_space=pl.ANY)
     return pl.pallas_call(
         kernel,
         out_shape=(
-            jax.ShapeDtypeStruct((128, W), BF16),
-            jax.ShapeDtypeStruct((128, W), BF16),
+            jax.ShapeDtypeStruct((chunks, m, W), BF16),
+            jax.ShapeDtypeStruct((chunks, m, W), BF16),
             jax.ShapeDtypeStruct((256, 2 * W), BF16),
             jax.ShapeDtypeStruct((W, W), BF16),
         ),
-        in_specs=[vmem, vmem, anywhere, vmem],
-        out_specs=(vmem,) * 4,
+        in_specs=[anywhere] * 4,
+        out_specs=(anywhere,) * 4,
         scratch_shapes=[
             pltpu.VMEM((chunks, 4, 4, m, W), BF16),
             pltpu.VMEM((chunks, 4, 4, m, W), BF16),
@@ -533,9 +566,12 @@
             pltpu.VMEM((chunks, 2, 3, m, W), BF16),
             pltpu.VMEM((2, W, W), F32),
             pltpu.VMEM((2, 256, W), BF16),
+            pltpu.VMEM((W, W), BF16),
+            pltpu.VMEM((2, 256, W), BF16),
+            pltpu.VMEM((W, W), BF16),
             pltpu.VMEM((2, 256, W), BF16),
             pltpu.VMEM((2, 256, W), BF16),
-            pltpu.VMEM((2, 256, W), BF16),
+            pltpu.VMEM((2, chunks, m, W), BF16),
             dma((chunks, 2, 2, 3)), dma((chunks, 2, 2, 3)),
             dma((chunks, 2)), dma((chunks, 2)),
             dma((chunks, 2, 3)), dma((chunks, 2, 3)),
@@ -543,6 +579,7 @@
             dma((chunks, 4)), dma((chunks, 4)),
             dma((chunks, 2, 2, 3)), dma((chunks, 2, 2, 3)),
             dma((2, 2, 2, pieces)), dma((2, 2, 2, pieces)),
+            dma((4,)), dma((2, chunks)),
         ],
         compiler_params=pltpu.CompilerParams(
             collective_id=0, has_side_effects=True, vmem_limit_bytes=56 << 20
@@ -550,11 +587,42 @@
         cost_estimate=pl.CostEstimate(
             flops=6 * 2 * 2048 * W * W, bytes_accessed=3 << 20, transcendentals=2048 * W
         ),
-    )(tokens, cotangent, weight_in, weight_out)
+    )(tokens.reshape(chunks, m, W), cotangent.reshape(chunks, m, W), weight_in, weight_out)
+
+
+def hand_over(*refs):
+    held, given, rooms, arrived, done = refs[:4], refs[4:8], refs[8:12], refs[12], refs[13]
+    ways = []
+    for i in range(4):
+        rows = held[i].shape[0] // parts_of_result
+        for j in range(parts_of_result):
+            part = pl.ds(j * rows, rows)
+            room = rooms[i].at[part]
+            ways.append((
+                pltpu.make_async_copy(held[i].at[part], room, arrived.at[i, j]),
+                pltpu.make_async_copy(room, given[i].at[part], done.at[i, j]),
+            ))
+    for come, _ in ways:
+        come.start()
+    for come, go in ways:
+        come.wait()
+        go.start()
+    for _, go in ways:
+        go.wait()
 
 
 def on_device(tokens, weight_in, weight_out, cotangent):
-    return fused(tokens, cotangent, weight_in, weight_out)
+    output, grad_tokens, grad_in, grad_out = fused(tokens, cotangent, weight_in, weight_out)
+    results = (output.reshape(128, W), grad_tokens.reshape(128, W), grad_in, grad_out)
+    anywhere = pl.BlockSpec(memory_space=pl.ANY)
+    return pl.pallas_call(
+        hand_over,
+        out_shape=[jax.ShapeDtypeStruct(r.shape, r.dtype) for r in results],
+        in_specs=[anywhere] * 4,
+        out_specs=[anywhere] * 4,
+        scratch_shapes=[pltpu.VMEM(r.shape, r.dtype) for r in results]
+        + [pltpu.SemaphoreType.DMA((4, parts_of_result))] * 2,
+    )(*results)
 
 
 def solution(mesh):

time: 111 us -> 102 us (0.919)
  local copies, waits for them, and re-layouts: 5.22 us -> 0 us
  Pallas kernels: 105 us -> 101 us
    unnamed x8 -> x0, local copies, waits for them, and re-layouts: 5.22 us -> none
    pallas_call x1 -> x2, Pallas kernels: 105 us -> 101 us  [the longest x1 98.7 us: fused(): pl.pallas_call(kernel, out_shape=(jax.ShapeDtypeStruct((chunks, m, W), BF...]
where the time goes in v2:
time: 102 us
  Pallas kernels  101 us (99%)
    pallas_call x1, Pallas kernels, fused(): pl.pallas_call(kernel, out_shape=(jax.ShapeDtypeStruct((chunks, m, W), BF...  98.7 us
    pallas_call x1, Pallas kernels, on_device(): pl.pallas_call(hand_over, out_shape=[jax.ShapeDtypeStruct(r.shape, r.dtyp...  2.19 us

profile of v2, /device:TPU:1, one launch (start us, length us, event | category | flops | bytes accessed | tf_op | source)
XLA Modules:
  0.0 101.5 jit_solution(11868589116620278484)
XLA Ops:
  0.6 98.7 %shard_map.75 = (bf16[8,16,512]{2,1,0:T(8,128)(2,1)}, bf16[8,16,512]{2,1,0:T(8,128)(2,1)}, bf16[256,1024]{1,0:T(8,128)(2,1)}, bf16[512,512]{1,0:T(8,128)(2,1)}) custom-call(bf16[8,16,512]{2,1,0:T(8,128)(2,1)} %bitcast.6, bf16[8,16,512]{2,1,0:T(8,128)(2,1)} %bitcast.7, bf16[256,1024]{1,0:T(8,128)(2,1)} %win_ref.1, bf16[512,512]{1,0:T(8,128)(2,1)} %wout_ref.1), custom_call_target="tpu_custom_call" | custom-call | flops 6442450944 | bytes 3145728 | tf_op jit(solution)/shard_map/pallas_call | solution.py:540
  99.3 2.2 %shard_map.76 = (bf16[128,512]{1,0:T(8,128)(2,1)}, bf16[128,512]{1,0:T(8,128)(2,1)}, bf16[256,1024]{1,0:T(8,128)(2,1)}, bf16[512,512]{1,0:T(8,128)(2,1)}) custom-call(bf16[128,512]{1,0:T(8,128)(2,1)} %bitcast.4, bf16[128,512]{1,0:T(8,128)(2,1)} %bitcast.5, bf16[256,1024]{1,0:T(8,128)(2,1)} %get-tuple-element.10.refs_2_, ...), custom_call_target="tpu_custom_call" | custom-call | tf_op jit(solution)/shard_map/pallas_call | solution.py:618

commit v3 on v2

--- a/solution.py
+++ b/solution.py
@@ -57,9 +57,9 @@
 def kernel(
     x_ref, c_ref, win_ref, wout_ref,
     out_ref, gx_ref, gw1_ref, gw2_ref,
-    ax, ac, part, ks, kr, zs, zt, zr, hg, os, gs, t1, r1, u, t2, r2, acc,
+    ax, ac, part, kr, zs, zt, zr, hg, os, gs, t1, r1, u, t2, r2, acc,
     w1, w2, gw1, gw2, stay, back, ready,
-    s_g, r_g, s_k, r_k, s_z, r_z, s_h, r_h, s_p, r_p, s_o, r_o, s_w, r_w, s_l, r_l,
+    s_g, r_g, s_k, r_k, s_z, r_z, s_h, r_h, s_p, r_p, s_o, r_o, r_q, s_w, r_w, r_t, s_l, r_l,
 ):
     row, col = lax.axis_index("row"), lax.axis_index("col")
     x, y, z, k = row // 4, lax.rem(row, 4), col // 2, lax.rem(col, 2)
@@ -135,31 +135,30 @@
             self.way, self.source, self.middle, self.target = way, source, middle, target
 
         def move_1(self, j, q):
-            where = (self.way, 0, j, q)
+            where = (self.way, j, q)
             rows = pl.ds(q * size, size)
             return copy(
-                self.source(j, rows), self.middle.at[j, rows], s_w.at[where], r_w.at[where],
+                self.source(j, rows), self.middle.at[j, rows], s_w.at[self.way, 0, j], r_w.at[where],
                 on_z(lax.rem(z + shift(2 * k + j), 4)),
             )
 
         def move_2(self, j, q, slot):
-            send, recv = (self.way, 1, j, q), (self.way, 1, slot, q)
             rows = pl.ds(q * size, size)
             return copy(
                 self.middle.at[j, rows], self.target(slot, rows),
-                s_w.at[send], r_w.at[recv], turn_target(2 * k + j),
+                s_w.at[self.way, 1, j], r_t.at[self.way], turn_target(2 * k + j),
             )
 
         def stay_1(self, j, q):
             rows = pl.ds(q * size, size)
             return pltpu.make_async_copy(
-                self.source(j, rows), self.middle.at[j, rows], r_w.at[self.way, 0, j, q]
+                self.source(j, rows), self.middle.at[j, rows], r_w.at[self.way, j, q]
             )
 
         def stay_2(self, j, q):
             rows = pl.ds(q * size, size)
             return pltpu.make_async_copy(
-                self.middle.at[j, rows], self.target(j, rows), r_w.at[self.way, 1, j, q]
+                self.middle.at[j, rows], self.target(j, rows), r_t.at[self.way]
             )
 
         def either(self, condition, yes, no):
@@ -186,18 +185,21 @@
                         lambda: self.move_2(j, q, slot).start(),
                     )
 
+        def whole(self, j, stage):
+            return copy(
+                self.middle.at[j], self.middle.at[j], s_w.at[self.way, stage, j],
+                r_t.at[self.way], partner,
+            )
+
         def wait_recv(self):
-            for q in range(pieces):
-                for slot in (0, 1):
-                    self.move_2(0, q, slot).wait_recv()
+            copy(
+                self.middle, self.middle, s_w.at[self.way, 0, 0], r_t.at[self.way], partner
+            ).wait_recv()
 
         def wait_send(self):
-            for q in range(pieces):
-                for j in (0, 1):
-                    pl.when(shift(2 * k + j) != 0)(lambda: self.move_1(j, q).wait_send())
-                    pl.when(jnp.logical_not(is_home(j)))(
-                        lambda: self.move_2(j, q, 0).wait_send()
-                    )
+            for j in (0, 1):
+                pl.when(shift(2 * k + j) != 0)(lambda: self.whole(j, 0).wait_send())
+                pl.when(jnp.logical_not(is_home(j)))(lambda: self.whole(j, 1).wait_send())
 
     def half(slot):
         return pl.ds(pl.multiple_of(slot * W, W), W)
@@ -210,14 +212,14 @@
     )
 
     class Gather:
-        def __init__(self, relay, region, place, here, sends, recvs):
+        def __init__(self, relay, region, place, here, send, recvs):
             self.relay, self.region, self.place, self.here = relay, region, place, here
-            self.sends, self.recvs = sends, recvs
+            self.send, self.recvs = send, recvs
 
         def move(self, p, step, to):
-            j = step % 4
+            first = self.relay and step == 1
             return copy(
-                self.region(p), self.region(p), self.sends.at[j - 1], self.recvs.at[j - 1],
+                self.region(p), self.region(p), self.send, self.recvs.at[1 if first else 0],
                 self.place(at(self.here, to)),
             )
 
@@ -234,24 +236,19 @@
                 self.move(behind, 2, 1).start()
 
         def wait_recv(self):
-            if not self.relay:
-                self.move(at(self.here, -1), 1, 1).wait_recv()
-            self.move(at(self.here, 1), 3, 1).wait_recv()
-            self.move(at(self.here, 2), 2, 1).wait_recv()
-
-        def wait_send(self):
-            for j in (1, 2, 3):
-                self.move(self.here, j, 1).wait_send()
+            blocks = self.region(pl.ds(0, 2 if self.relay else 3))
+            copy(blocks, blocks, self.send, self.recvs.at[0], partner).wait_recv()
 
     class Scatter:
-        def __init__(self, relay, source, held, got, place, here, sends, recvs):
+        def __init__(self, relay, source, held, got, place, here, send, recvs):
             self.relay, self.source, self.held, self.got = relay, source, held, got
-            self.place, self.here, self.sends, self.recvs = place, here, sends, recvs
+            self.place, self.here, self.send, self.recvs = place, here, send, recvs
 
         def move(self, src, step, to):
-            j = step % 4
+            slot = {2: 0, 3: 1, 1: 2}[step]
+            first = self.relay and step == 2
             return copy(
-                src, self.got.at[j - 1], self.sends.at[j - 1], self.recvs.at[j - 1],
+                src, self.got.at[slot], self.send, self.recvs.at[1 if first else 0],
                 self.place(at(self.here, to)),
             )
 
@@ -261,54 +258,48 @@
             if not self.relay:
                 self.move(self.source(at(self.here, 1)), 1, 1).start()
 
-        def wait(self, j):
-            self.move(self.source(self.here), j, 1).wait_recv()
-            return self.got[j - 1].astype(F32)
-
-        def forward(self):
+        def forward(self, own):
             if self.relay:
-                value = self.source(at(self.here, 1))[...].astype(F32) + self.wait(2)
-                self.held[...] = value.astype(BF16)
+                self.move(self.source(self.here), 2, 1).wait_recv()
+                self.held[...] = (own + self.got[0].astype(F32)).astype(BF16)
                 self.move(self.held, 1, 1).start()
 
         def total(self, own):
-            for j in (3, 1) if self.relay else (1, 3, 2):
-                own = own + self.wait(j)
+            blocks = self.got.at[pl.ds(1, 2)] if self.relay else self.got
+            copy(blocks, blocks, self.send, self.recvs.at[0], partner).wait_recv()
+            for slot in (1, 2) if self.relay else (0, 1, 2):
+                own = own + self.got[slot].astype(F32)
             return own
-
-        def wait_send(self):
-            for j in (1, 2, 3):
-                self.move(self.source(self.here), j, 1).wait_send()
 
     def gather_x(i, phase):
         region = (lambda p: ax.at[i, p, y]) if phase == 0 else (lambda p: ax.at[i, :, p])
         place, here = ((on_x, x), (on_y, y))[phase]
         relay = (relay_gather_1, relay_gather_2)[phase]
-        return Gather(relay, region, place, here, s_g.at[i, phase, 0], r_g.at[i, phase, 0])
+        return Gather(relay, region, place, here, s_g.at[phase, 0], r_g.at[i, phase, 0])
 
     def gather_c(i, phase):
         region = (lambda p: ac.at[i, x, p]) if phase == 0 else (lambda p: ac.at[i, p])
         place, here = ((on_y, y), (on_x, x))[phase]
         relay = (relay_gather_1, relay_gather_2)[phase]
-        return Gather(relay, region, place, here, s_g.at[i, phase, 1], r_g.at[i, phase, 1])
+        return Gather(relay, region, place, here, s_g.at[phase, 1], r_g.at[i, phase, 1])
 
     def gather_h(i):
         return Gather(
-            relay_gather_z, lambda p: hg.at[i, :, k, p], on_z, z, s_h.at[i], r_h.at[i]
+            relay_gather_z, lambda p: hg.at[i, :, k, p], on_z, z, s_h.at[0], r_h.at[i]
         )
 
     def exchange(i, w):
-        return copy(ks.at[i, w], kr.at[i, w], s_k.at[i, w], r_k.at[i, w], partner)
+        return copy(part.at[i, w, 1 - k], kr.at[i, w], s_k.at[w], r_k.at[i, w], partner)
 
     def scatter_z(i, w):
         return Scatter(
             relay_sum_z, lambda p: zs.at[i, w, p], zt.at[i, w], zr.at[i, w], on_z, z,
-            s_z.at[i, w], r_z.at[i, w],
+            s_z.at[w], r_z.at[i, w],
         )
 
-    def pair(i, j, p, core):
+    def pair(i, p):
         return copy(
-            hg.at[i, :, core, p], hg.at[i, :, core, p], s_p.at[i, j], r_p.at[i, j], partner
+            hg.at[i, :, k, p], hg.at[i, :, k, p], s_p.at[0], r_p.at[i], partner
         )
 
     def scatter_1(i, a):
@@ -316,14 +307,14 @@
         place, here = ((on_y, y), (on_x, x))[a]
         return Scatter(
             relay_sum_1, source, t1.at[i, a], r1.at[i, a], place, here,
-            s_o.at[i, 0, a], r_o.at[i, 0, a],
+            s_o.at[0, a], r_o.at[i, a],
         )
 
     def scatter_2(i, a):
         place, here = ((on_x, x), (on_y, y))[a]
         return Scatter(
             relay_sum_2, lambda p: u.at[i, a, p], t2.at[i, a], r2.at[i, a], place, here,
-            s_o.at[i, 1, a], r_o.at[i, 1, a],
+            s_o.at[1, a], r_q.at[i, pl.ds(a, 1)],
         )
 
     def gather_1x(i):
@@ -348,8 +339,10 @@
 
     def give(i, w, product):
         part[i, w] = product.reshape(2, 4, tz, W)
-        ks[i, w] = part[i, w, 1 - k]
         exchange(i, w).start()
+
+    def mixed(i, w, p):
+        return part[i, w, k, p] + kr[i, w, p]
 
     def multiply_g(i):
         @pl.when(i == 0)
@@ -369,9 +362,8 @@
 
     def sum_z(i, w):
         exchange(i, w).wait_recv()
-        part[i, w, k] += kr[i, w]
         for p in range(4):
-            zs[i, w, p] = part[i, w, k, p].astype(BF16)
+            zs[i, w, p] = mixed(i, w, p).astype(BF16)
         scatter_z(i, w).start()
 
     def sum_z_p(i):
@@ -381,36 +373,34 @@
         sum_z(i, 1)
 
     def sum_z_p_relay(i):
-        scatter_z(i, 0).forward()
+        scatter_z(i, 0).forward(mixed(i, 0, at(z, 1)))
 
     def sum_z_g_relay(i):
-        scatter_z(i, 1).forward()
+        scatter_z(i, 1).forward(mixed(i, 1, at(z, 1)))
 
     def activate(i):
-        grad = scatter_z(i, 1).total(part[i, 1, k, z])
-        hidden, slope = activate_both(scatter_z(i, 0).total(part[i, 0, k, z]))
+        grad = scatter_z(i, 1).total(mixed(i, 1, z))
+        hidden, slope = activate_both(scatter_z(i, 0).total(mixed(i, 0, z)))
         hg[i, 0, k, z] = hidden.astype(BF16)
         hg[i, 1, k, z] = (grad * slope).astype(BF16)
         gather_h(i).start()
-        pair(i, 0, z, k).start()
+        pair(i, z).start()
 
     def gather_z_relay(i):
         gather_h(i).forward()
         if relay_gather_z:
-            pair(i, 1, at(z, -1), k).start()
+            pair(i, at(z, -1)).start()
 
     def gather_z(i):
         gather_h(i).wait_recv()
         if not relay_gather_z:
-            pair(i, 1, at(z, -1), k).start()
-        pair(i, 2, at(z, 1), k).start()
-        pair(i, 3, at(z, 2), k).start()
+            pair(i, at(z, -1)).start()
+        pair(i, at(z, 1)).start()
+        pair(i, at(z, 2)).start()
 
     def multiply_w(i):
-        pair(i, 0, z, 1 - k).wait_recv()
-        pair(i, 1, at(z, 1), 1 - k).wait_recv()
-        pair(i, 2, at(z, -1), 1 - k).wait_recv()
-        pair(i, 3, at(z, 2), 1 - k).wait_recv()
+        others = hg.at[i, :, 1 - k]
+        copy(others, others, s_p.at[0], r_p.at[i], partner).wait_recv()
         acc[0] += dot_tn(ax[i].reshape(n, W), hg[i, 1].reshape(n, W))
 
         @pl.when(i == chunks - 1)
@@ -432,10 +422,10 @@
         acc[1] += dot_tn(hg[i, 0].reshape(n, W), ac[i].reshape(n, W))
 
     def sum_1o_relay(i):
-        scatter_1(i, 0).forward()
+        scatter_1(i, 0).forward(os[i, :, at(y, 1)].astype(F32))
 
     def sum_1x_relay(i):
-        scatter_1(i, 1).forward()
+        scatter_1(i, 1).forward(gs[i, at(x, 1)].astype(F32))
 
     def sum_2o(i):
         u[i, 0] = scatter_1(i, 0).total(os[i, :, y].astype(F32)).astype(BF16)
@@ -446,7 +436,7 @@
         scatter_2(i, 1).start()
 
     def keep(i, a):
-        return pltpu.make_async_copy(ready.at[a, i], (out_ref, gx_ref)[a].at[i], r_l.at[a, i])
+        return pltpu.make_async_copy(ready.at[a, i], (out_ref, gx_ref)[a].at[i], r_l.at[a])
 
     def store_o(i):
         ready[0, i] = scatter_2(i, 0).total(u[i, 0, x].astype(F32)).astype(BF16)
@@ -512,25 +502,24 @@
     gw2[...] = acc[1].astype(BF16)
     keep_w.start()
 
-    def drain(i, _):
-        for phase in (0, 1):
-            gather_x(i, phase).wait_send()
-            gather_c(i, phase).wait_send()
-        gather_h(i).wait_send()
-        for a in (0, 1):
-            keep(i, a).wait()
-            exchange(i, a).wait_send()
-            scatter_z(i, a).wait_send()
-            scatter_1(i, a).wait_send()
-            scatter_2(i, a).wait_send()
-        for j in range(4):
-            pair(i, j, z, k).wait_send()
-        return 0
-
-    lax.fori_loop(0, chunks, drain, 0)
+    def sent(blocks, semaphore):
+        copy(blocks, blocks, semaphore, r_t.at[0], partner).wait_send()
+
+    most = 3 * chunks // 4
+    for a, all_blocks in ((0, ax), (1, ac)):
+        sent(all_blocks.at[pl.ds(0, most), 0], s_g.at[0, a])
+        sent(all_blocks.at[pl.ds(0, most)], s_g.at[1, a])
+        sent(kr.at[:, a], s_k.at[a])
+        sent(zr.at[:, a], s_z.at[a])
+        sent(r1.at[:, a], s_o.at[0, a])
+        sent(r2.at[:, a], s_o.at[1, a])
+    sent(hg.at[pl.ds(0, most), :, 0], s_h.at[0])
+    sent(hg.at[:, 0], s_p.at[0])
     turn_in.wait_send()
     turn_out.wait_recv()
     turn_out.wait_send()
+    for a in (0, 1):
+        pltpu.make_async_copy(ready.at[a], (out_ref, gx_ref)[a], r_l.at[a]).wait()
     keep_w.wait()
 
 
@@ -551,7 +540,6 @@
             pltpu.VMEM((chunks, 4, 4, m, W), BF16),
             pltpu.VMEM((chunks, 4, 4, m, W), BF16),
             pltpu.VMEM((chunks, 2, 2, 4, tz, W), F32),
-            pltpu.VMEM((chunks, 2, 4, tz, W), F32),
             pltpu.VMEM((chunks, 2, 4, tz, W), F32),
             pltpu.VMEM((chunks, 2, 4, tz, W), BF16),
             pltpu.VMEM((chunks, 2, tz, W), BF16),
@@ -572,14 +560,14 @@
             pltpu.VMEM((2, 256, W), BF16),
             pltpu.VMEM((2, 256, W), BF16),
             pltpu.VMEM((2, chunks, m, W), BF16),
-            dma((chunks, 2, 2, 3)), dma((chunks, 2, 2, 3)),
-            dma((chunks, 2)), dma((chunks, 2)),
-            dma((chunks, 2, 3)), dma((chunks, 2, 3)),
-            dma((chunks, 3)), dma((chunks, 3)),
-            dma((chunks, 4)), dma((chunks, 4)),
-            dma((chunks, 2, 2, 3)), dma((chunks, 2, 2, 3)),
-            dma((2, 2, 2, pieces)), dma((2, 2, 2, pieces)),
-            dma((4,)), dma((2, chunks)),
+            dma((2, 2)), dma((chunks, 2, 2, 1 + max(relay_gather_1, relay_gather_2))),
+            dma((2,)), dma((chunks, 2)),
+            dma((2,)), dma((chunks, 2, 2)),
+            dma((1,)), dma((chunks, 2)),
+            dma((1,)), dma((chunks,)),
+            dma((2, 2)), dma((chunks, 2, 2)), dma((chunks, 2)),
+            dma((2, 2, 2)), dma((2, 2, pieces)), dma((2,)),
+            dma((4,)), dma((2,)),
         ],
         compiler_params=pltpu.CompilerParams(
             collective_id=0, has_side_effects=True, vmem_limit_bytes=56 << 20

time: 102 us -> 97.3 us (0.954)
  Pallas kernels: 101 us -> 96.2 us
    pallas_call x1, Pallas kernels: 98.7 us -> 94 us  [fused(): pl.pallas_call(kernel, out_shape=(jax.ShapeDtypeStruct((chunks, m, W), BF...]
where the time goes in v3:
time: 97.3 us; the launch traced here: 96.8 us
  Pallas kernels  96.2 us (99%)
    pallas_call x1, Pallas kernels, fused(): pl.pallas_call(kernel, out_shape=(jax.ShapeDtypeStruct((chunks, m, W), BF...  94 us
    pallas_call x1, Pallas kernels, on_device(): pl.pallas_call(hand_over, out_shape=[jax.ShapeDtypeStruct(r.shape, r.dtyp...  2.19 us

profile of v3, /device:TPU:1, one launch (start us, length us, event | category | flops | bytes accessed | tf_op | source)
XLA Modules:
  0.0 96.8 jit_solution(16512133039494005171)
XLA Ops:
  0.6 94.0 %shard_map.75 = (bf16[8,16,512]{2,1,0:T(8,128)(2,1)}, bf16[8,16,512]{2,1,0:T(8,128)(2,1)}, bf16[256,1024]{1,0:T(8,128)(2,1)}, bf16[512,512]{1,0:T(8,128)(2,1)}) custom-call(bf16[8,16,512]{2,1,0:T(8,128)(2,1)} %bitcast.6, bf16[8,16,512]{2,1,0:T(8,128)(2,1)} %bitcast.7, bf16[256,1024]{1,0:T(8,128)(2,1)} %win_ref.1, bf16[512,512]{1,0:T(8,128)(2,1)} %wout_ref.1), custom_call_target="tpu_custom_call" | custom-call | flops 6442450944 | bytes 3145728 | tf_op jit(solution)/shard_map/pallas_call | solution.py:529
  94.6 2.2 %shard_map.76 = (bf16[128,512]{1,0:T(8,128)(2,1)}, bf16[128,512]{1,0:T(8,128)(2,1)}, bf16[256,1024]{1,0:T(8,128)(2,1)}, bf16[512,512]{1,0:T(8,128)(2,1)}) custom-call(bf16[128,512]{1,0:T(8,128)(2,1)} %bitcast.4, bf16[128,512]{1,0:T(8,128)(2,1)} %bitcast.5, bf16[256,1024]{1,0:T(8,128)(2,1)} %get-tuple-element.10.refs_2_, ...), custom_call_target="tpu_custom_call" | custom-call | tf_op jit(solution)/shard_map/pallas_call | solution.py:606

commit v4 on v3

--- a/solution.py
+++ b/solution.py
@@ -21,7 +21,7 @@
 tz = n // 8
 W = 512
 parts_of_result = 2
-pieces = 4
+pieces = 8
 
 relay_gather_1, relay_gather_2 = False, False
 relay_sum_z, relay_gather_z = True, True
@@ -58,15 +58,20 @@
     x_ref, c_ref, win_ref, wout_ref,
     out_ref, gx_ref, gw1_ref, gw2_ref,
     ax, ac, part, kr, zs, zt, zr, hg, os, gs, t1, r1, u, t2, r2, acc,
-    w1, w2, gw1, gw2, stay, back, ready,
+    w1, w2, gw1, gw2, stay, back, ready, whole, kept,
     s_g, r_g, s_k, r_k, s_z, r_z, s_h, r_h, s_p, r_p, s_o, r_o, r_q, s_w, r_w, r_t, s_l, r_l,
 ):
     row, col = lax.axis_index("row"), lax.axis_index("col")
     x, y, z, k = row // 4, lax.rem(row, 4), col // 2, lax.rem(col, 2)
     sign = 1 - 2 * k
 
-    def at(base, step):
-        return lax.rem(base + step * sign + 4, 4)
+    rings = {
+        id(here): [lax.rem(here + step * sign + 4, 4) for step in (0, 1, 2, -1)]
+        for here in (x, y, z)
+    }
+
+    def at(here, step):
+        return rings[id(here)][step % 4]
 
     def on_x(p):
         return (p * 4 + y, col)
@@ -410,11 +415,13 @@
 
     def multiply_o(i):
         product = dot_nn(hg[i, 0].reshape(n, W), w2[...])
+        whole[i, 0] = product.reshape(4, 4, m, W)
         os[i] = product.astype(BF16).reshape(4, 4, m, W)
         scatter_1(i, 0).start()
 
     def multiply_x(i):
         product = dot_nt(hg[i, 1].reshape(n, W), w1[...].reshape(W, W))
+        whole[i, 1] = product.reshape(4, 4, m, W)
         gs[i] = product.astype(BF16).reshape(4, 4, m, W)
         scatter_1(i, 1).start()
 
@@ -422,28 +429,32 @@
         acc[1] += dot_tn(hg[i, 0].reshape(n, W), ac[i].reshape(n, W))
 
     def sum_1o_relay(i):
-        scatter_1(i, 0).forward(os[i, :, at(y, 1)].astype(F32))
+        scatter_1(i, 0).forward(whole[i, 0, :, at(y, 1)])
 
     def sum_1x_relay(i):
-        scatter_1(i, 1).forward(gs[i, at(x, 1)].astype(F32))
+        scatter_1(i, 1).forward(whole[i, 1, at(x, 1)])
 
     def sum_2o(i):
-        u[i, 0] = scatter_1(i, 0).total(os[i, :, y].astype(F32)).astype(BF16)
+        total = scatter_1(i, 0).total(whole[i, 0, :, y])
+        kept[i, 0] = total
+        u[i, 0] = total.astype(BF16)
         scatter_2(i, 0).start()
 
     def sum_2x(i):
-        u[i, 1] = scatter_1(i, 1).total(gs[i, x].astype(F32)).astype(BF16)
+        total = scatter_1(i, 1).total(whole[i, 1, x])
+        kept[i, 1] = total
+        u[i, 1] = total.astype(BF16)
         scatter_2(i, 1).start()
 
     def keep(i, a):
         return pltpu.make_async_copy(ready.at[a, i], (out_ref, gx_ref)[a].at[i], r_l.at[a])
 
     def store_o(i):
-        ready[0, i] = scatter_2(i, 0).total(u[i, 0, x].astype(F32)).astype(BF16)
+        ready[0, i] = scatter_2(i, 0).total(kept[i, 0, x]).astype(BF16)
         keep(i, 0).start()
 
     def store_x(i):
-        ready[1, i] = scatter_2(i, 1).total(u[i, 1, y].astype(F32)).astype(BF16)
+        ready[1, i] = scatter_2(i, 1).total(kept[i, 1, y]).astype(BF16)
         keep(i, 1).start()
 
     def turn_in_relay(i):
@@ -560,6 +571,8 @@
             pltpu.VMEM((2, 256, W), BF16),
             pltpu.VMEM((2, 256, W), BF16),
             pltpu.VMEM((2, chunks, m, W), BF16),
+            pltpu.VMEM((chunks, 2, 4, 4, m, W), F32),
+            pltpu.VMEM((chunks, 2, 4, m, W), F32),
             dma((2, 2)), dma((chunks, 2, 2, 1 + max(relay_gather_1, relay_gather_2))),
             dma((2,)), dma((chunks, 2)),
             dma((2,)), dma((chunks, 2, 2)),
@@ -570,7 +583,7 @@
             dma((4,)), dma((2,)),
         ],
         compiler_params=pltpu.CompilerParams(
-            collective_id=0, has_side_effects=True, vmem_limit_bytes=56 << 20
+            collective_id=0, has_side_effects=True, vmem_limit_bytes=58 << 20
         ),
         cost_estimate=pl.CostEstimate(
             flops=6 * 2 * 2048 * W * W, bytes_accessed=3 << 20, transcendentals=2048 * W

time: 97.3 us -> 97 us (level)
  no operation moved by 1% of the time
where the time goes in v4:
time: 97 us; the launch traced here: 96.8 us
  Pallas kernels  96.2 us (99%)
    pallas_call x1, Pallas kernels, fused(): pl.pallas_call(kernel, out_shape=(jax.ShapeDtypeStruct((chunks, m, W), BF...  94 us
    pallas_call x1, Pallas kernels, on_device(): pl.pallas_call(hand_over, out_shape=[jax.ShapeDtypeStruct(r.shape, r.dtyp...  2.19 us

profile of v4, /device:TPU:1, one launch (start us, length us, event | category | flops | bytes accessed | tf_op | source)
XLA Modules:
  0.0 96.8 jit_solution(9712919965158745476)
XLA Ops:
  0.6 94.0 %shard_map.75 = (bf16[8,16,512]{2,1,0:T(8,128)(2,1)}, bf16[8,16,512]{2,1,0:T(8,128)(2,1)}, bf16[256,1024]{1,0:T(8,128)(2,1)}, bf16[512,512]{1,0:T(8,128)(2,1)}) custom-call(bf16[8,16,512]{2,1,0:T(8,128)(2,1)} %bitcast.6, bf16[8,16,512]{2,1,0:T(8,128)(2,1)} %bitcast.7, bf16[256,1024]{1,0:T(8,128)(2,1)} %win_ref.1, bf16[512,512]{1,0:T(8,128)(2,1)} %wout_ref.1), custom_call_target="tpu_custom_call" | custom-call | flops 6442450944 | bytes 3145728 | tf_op jit(solution)/shard_map/pallas_call | solution.py:540
  94.6 2.2 %shard_map.76 = (bf16[128,512]{1,0:T(8,128)(2,1)}, bf16[128,512]{1,0:T(8,128)(2,1)}, bf16[256,1024]{1,0:T(8,128)(2,1)}, bf16[512,512]{1,0:T(8,128)(2,1)}) custom-call(bf16[128,512]{1,0:T(8,128)(2,1)} %bitcast.4, bf16[128,512]{1,0:T(8,128)(2,1)} %bitcast.5, bf16[256,1024]{1,0:T(8,128)(2,1)} %get-tuple-element.10.refs_2_, ...), custom_call_target="tpu_custom_call" | custom-call | tf_op jit(solution)/shard_map/pallas_call | solution.py:619

commit v5 on v4

--- a/solution.py
+++ b/solution.py
@@ -481,13 +481,13 @@
         (9, multiply_p),
         (24, sum_2x),
         (9, multiply_g),
-        (41, store_o),
+        (31, store_o),
         (19, sum_1x_relay),
         (20, turn_out_relay),
         (6, gather_2x),
         (9, sum_z_p),
         (9, sum_z_g),
-        (37, store_x),
+        (30, store_x),
         (15, gather_z),
         (1, gather_1c),
         (10, sum_z_p_relay),

time: 97 us -> 96.4 us (level)
  no operation moved by 1% of the time
where the time goes in v5:
time: 96.4 us; the launch traced here: 96.1 us
  Pallas kernels  95.5 us (99%)
    pallas_call x1, Pallas kernels, fused(): pl.pallas_call(kernel, out_shape=(jax.ShapeDtypeStruct((chunks, m, W), BF...  93.3 us
    pallas_call x1, Pallas kernels, on_device(): pl.pallas_call(hand_over, out_shape=[jax.ShapeDtypeStruct(r.shape, r.dtyp...  2.19 us

profile of v5, /device:TPU:1, one launch (start us, length us, event | category | flops | bytes accessed | tf_op | source)
XLA Modules:
  0.0 96.1 jit_solution(13954743682351306356)
XLA Ops:
  0.6 93.3 %shard_map.75 = (bf16[8,16,512]{2,1,0:T(8,128)(2,1)}, bf16[8,16,512]{2,1,0:T(8,128)(2,1)}, bf16[256,1024]{1,0:T(8,128)(2,1)}, bf16[512,512]{1,0:T(8,128)(2,1)}) custom-call(bf16[8,16,512]{2,1,0:T(8,128)(2,1)} %bitcast.6, bf16[8,16,512]{2,1,0:T(8,128)(2,1)} %bitcast.7, bf16[256,1024]{1,0:T(8,128)(2,1)} %win_ref.1, bf16[512,512]{1,0:T(8,128)(2,1)} %wout_ref.1), custom_call_target="tpu_custom_call" | custom-call | flops 6442450944 | bytes 3145728 | tf_op jit(solution)/shard_map/pallas_call | solution.py:540
  93.9 2.2 %shard_map.76 = (bf16[128,512]{1,0:T(8,128)(2,1)}, bf16[128,512]{1,0:T(8,128)(2,1)}, bf16[256,1024]{1,0:T(8,128)(2,1)}, bf16[512,512]{1,0:T(8,128)(2,1)}) custom-call(bf16[128,512]{1,0:T(8,128)(2,1)} %bitcast.4, bf16[128,512]{1,0:T(8,128)(2,1)} %bitcast.5, bf16[256,1024]{1,0:T(8,128)(2,1)} %get-tuple-element.10.refs_2_, ...), custom_call_target="tpu_custom_call" | custom-call | tf_op jit(solution)/shard_map/pallas_call | solution.py:619
